TPU v7x, 256 devices: a whole 4x4x8 slice. The times are simulated.
256 devices in a mesh: dp: 2 (over z_hi), mode: 16 (over x, z_lo), tm: 8 (over y, core).
Axes of the slice: x: 4, y: 4, z: 8 (z_hi: 2, z_lo: 4; z = z_hi * 4 + z_lo), core: 2. Of those that a mesh axis runs over, the one named last changes fastest.
Arguments:
- input_field: float32 [2, 16, 32, 16384], P(None, 'dp', 'mode', 'tm'), parts along dimension 1, may hold values from -6 to 6
- target_field: float32 [2, 16, 32, 16384], P(None, 'dp', 'mode', 'tm'), parts along dimension 1, may hold values from -6 to 6
- margin: float32 [32, 32, 16], P('mode'), may hold values from -0.25 to 0.25
- pair_index: int32 [16, 2], replicated, may hold values from 0 to 31
- mode_beta: float32 [1024, 32, 3], P(None, 'mode'), may hold values from -2 to 2
- segment_kind: int32 [1], replicated, may hold values from 0 to 1023
Outputs:
- field_gradient: float32 [2, 16, 32, 16384], P(None, 'dp', 'mode', 'tm'), parts along dimension 1
There are 2 independent parts, one for each index of `dp`. A program takes and returns all parts, laid end to end along the dimension named above; an argument that names none is the same for every part. Nothing has to cross between parts.
All inputs are finite; a program needn't handle non-finite values.
Results may differ from a plain program's by a relative error of at most 0.00011.
Values sent between devices are 32-bit elements; how exact they have to be, the bound alone decides.
No kernel may reach another device: no remote copies, remote signals or barrier semaphores. Data moves between devices by JAX's collectives and lax.ppermute only.
A program may use at most 128 MiB of HBM per device.

v0:
```python
import jax
import jax.numpy as jnp
import numpy as np
from jax import lax
from jax.experimental import pallas as pl
from jax.experimental.pallas import tpu as pltpu
from jax.sharding import PartitionSpec as P

f32, bf16 = jnp.float32, jnp.bfloat16
kerr_scale = 0.1
SIDE = 128
TOTAL = SIDE * SIDE
MODES, PAIRS = 32, 16
OWNERS = 16
TIMES = 8
BLOCK = 72


def dft_parts():
    a = np.arange(SIDE)
    angle = 2.0 * np.pi * (np.outer(a, a) % SIDE) / SIDE
    parts = []
    for table in (np.cos(angle), np.sin(angle)):
        head = table.astype(np.float32).astype(bf16)
        parts += [head, (table - head.astype(np.float64)).astype(np.float32).astype(bf16)]
    return np.stack(parts)


def twist_parts():
    a = np.arange(SIDE)
    angle = 2.0 * np.pi * np.outer(a, a) / TOTAL
    return np.stack([np.cos(angle), np.sin(angle)]).astype(np.float32)


def heads(x):
    head = x.astype(bf16)
    return head, (x - head.astype(f32)).astype(bf16)


def dot(a, b):
    return jnp.dot(a, b, preferred_element_type=f32)


def real_form(cos, sin):
    return jnp.concatenate(
        [jnp.concatenate([cos, sin], 1), jnp.concatenate([-sin, cos], 1)], 0
    )


def disperse_modes(series, dft, twist, phase, sign):
    ch, cl, sh, sl = (dft[q] for q in range(4))
    plus = (real_form(ch, sh), real_form(cl, sl))
    minus = (real_form(ch, -sh), real_form(cl, -sl))

    def left(form, x):
        head, rest = heads(x)
        return dot(
            jnp.concatenate([form[0], form[0], form[1]], 1),
            jnp.concatenate([head, rest, head], 0),
        )

    def right(form, x):
        head, rest = heads(x)
        return dot(
            jnp.concatenate([head, rest, head], 1),
            jnp.concatenate([form[0], form[0], form[1]], 0),
        )

    tc, ts = twist[0], twist[1]
    result = []
    for m, (re, im) in enumerate(series):
        pc, ps = phase[0, m], sign * phase[1, m]
        y = left(plus, jnp.concatenate([re, im], 0))
        yr, yi = y[:SIDE], y[SIDE:]
        y = jnp.concatenate([yr * tc + yi * ts, yi * tc - yr * ts], 1)
        z = right(minus, y)
        zr, zi = z[:, :SIDE], z[:, SIDE:]
        z = jnp.concatenate([zr * pc - zi * ps, zr * ps + zi * pc], 1)
        y = right(plus, z)
        yr, yi = y[:, :SIDE], y[:, SIDE:]
        y = jnp.concatenate([yr * tc - yi * ts, yr * ts + yi * tc], 0)
        x = left(minus, y)
        result.append((x[:SIDE], x[SIDE:]))
    return result


def forward_kernel(rows_ref, margin_ref, dft_ref, twist_ref, phase_ref, out_ref):
    def series(what, m, part):
        return [
            rows_ref[pl.ds(s * 128 + what * 64 + part * 32 + m, 16, stride=2), :]
            for s in range(TIMES)
        ]

    fields = [
        tuple(jnp.concatenate(series(0, m, part), 0) for part in range(2)) for m in range(2)
    ]
    for m in range(2):
        for part in range(2):
            for s, chunk in enumerate(series(1, m, part)):
                for h in range(2):
                    spot = (2 * s + h) * BLOCK + 32 + m * 16 + part * 8
                    out_ref[spot : spot + 8, :] = chunk[8 * h : 8 * h + 8]
    margin = margin_ref[...]
    for k in range(OWNERS):
        out_ref[k * BLOCK + 64 : k * BLOCK + 72, :] = margin
    result = disperse_modes(fields, dft_ref, twist_ref, phase_ref, 1.0)
    for m in range(2):
        for part in range(2):
            for k in range(OWNERS):
                spot = k * BLOCK + m * 16 + part * 8
                out_ref[spot : spot + 8, :] = result[m][part][8 * k : 8 * k + 8]


def backward_kernel(rows_ref, dft_ref, twist_ref, phase_ref, out_ref):
    fields = [
        tuple(
            jnp.concatenate(
                [
                    rows_ref[k * 32 + m * 16 + part * 8 : k * 32 + m * 16 + part * 8 + 8, :]
                    for k in range(OWNERS)
                ],
                0,
            )
            for part in range(2)
        )
        for m in range(2)
    ]
    result = disperse_modes(fields, dft_ref, twist_ref, phase_ref, -1.0)
    for m in range(2):
        for part in range(2):
            for s in range(TIMES):
                out_ref[pl.ds(s * 64 + part * 32 + m, 16, stride=2), :] = result[m][part][
                    16 * s : 16 * s + 16
                ]


def kerr_kernel(pair_ref, rows_ref, out_ref, w_ref, gw_ref):
    def by_owner(row):
        return rows_ref[pl.ds(row, OWNERS, stride=BLOCK), :]

    def modes_at(first, part, s):
        return jnp.concatenate(
            [by_owner(first + m * 16 + part * 8 + s) for m in range(2)], 0
        )

    def own_mode(mode, block):
        spot = (mode >> 1) * block + (mode & 1) * 16
        return pl.ds(pl.multiple_of(spot, 8), 16)

    lane = lax.broadcasted_iota(jnp.int32, (128, 128), 1)

    def stacked(x):
        head = x.astype(bf16).astype(f32)
        return jnp.where(lane < 64, head, x - head).astype(bf16)

    quarters = [
        jnp.concatenate([by_owner(64 + m * 4 + q) for m in range(2)], 0) for q in range(4)
    ]
    whole = jnp.concatenate(quarters, 0)
    first_form = []
    for jr in range(4):
        mine = jnp.where(lane // 32 == jr, whole, 0.0)
        mine = mine + pltpu.roll(mine, 64, 1)
        mine = mine + pltpu.roll(mine, 32, 1)
        first_form.append(stacked(mine))
    first_form = jnp.concatenate(first_form, 0)
    second_form = jnp.concatenate(
        [stacked(jnp.concatenate([q] * 4, 0).T) for q in quarters], 0
    )

    for j in range(PAIRS):
        left = rows_ref[own_mode(pair_ref[j, 0], BLOCK), :]
        right = rows_ref[own_mode(pair_ref[j, 1], BLOCK), :]
        lr, li, rr, ri = left[:8], left[8:], right[:8], right[8:]
        w_ref[j * 16 : j * 16 + 8, :] = lr * rr - li * ri
        w_ref[j * 16 + 8 : j * 16 + 16, :] = lr * ri + li * rr

    def operand(re, im):
        head, rest = heads(jnp.concatenate([re, im], 1))
        return jnp.concatenate([head, rest, head, rest], 0)

    for s in range(8):
        ur, ui = modes_at(0, 0, s), modes_at(0, 1, s)
        coupled = dot(first_form, operand(ur, ui))
        total_re = total_im = 0.0
        for j in range(PAIRS):
            row = ((j % 4) * 4 + j // 4) * 32
            cr, ci = coupled[row : row + 32, :128], coupled[row : row + 32, 128:]
            wr = w_ref[j * 16 + s : j * 16 + s + 1, :]
            wi = w_ref[j * 16 + 8 + s : j * 16 + 9 + s, :]
            total_re += cr * wr + ci * wi
            total_im += cr * wi - ci * wr
        gr = 2.0 * (ur - kerr_scale * total_im - modes_at(32, 0, s))
        gi = 2.0 * (ui + kerr_scale * total_re - modes_at(32, 1, s))
        spread = dot(second_form, operand(kerr_scale * gi, -kerr_scale * gr))
        for j in range(PAIRS):
            sr, si = spread[j * 32 : j * 32 + 32, :128], spread[j * 32 : j * 32 + 32, 128:]
            wr = w_ref[j * 16 + s : j * 16 + s + 1, :]
            wi = w_ref[j * 16 + 8 + s : j * 16 + 9 + s, :]
            gr += sr * wr + si * wi
            gi += sr * wi - si * wr
            gw_ref[j * 16 + s : j * 16 + s + 1, :] = jnp.sum(
                sr * ur - si * ui, axis=0, keepdims=True
            )
            gw_ref[j * 16 + 8 + s : j * 16 + 9 + s, :] = jnp.sum(
                sr * ui + si * ur, axis=0, keepdims=True
            )
        for m in range(2):
            for part, g in enumerate((gr, gi)):
                out_ref[pl.ds(m * 16 + part * 8 + s, OWNERS, stride=32), :] = g[
                    m * 16 : m * 16 + 16
                ]

    for j in range(PAIRS):
        gwr, gwi = gw_ref[j * 16 : j * 16 + 8, :], gw_ref[j * 16 + 8 : j * 16 + 16, :]
        for here, other in ((0, 1), (1, 0)):
            factor = rows_ref[own_mode(pair_ref[j, other], BLOCK), :]
            fr, fi = factor[:8], factor[8:]
            spot = own_mode(pair_ref[j, here], 32)
            out_ref[spot, :] = out_ref[spot, :] + jnp.concatenate(
                [gwr * fr + gwi * fi, gwi * fr - gwr * fi], 0
            )


def call(kernel, rows, *args, scratch=(), specs=None):
    vmem = pl.BlockSpec(memory_space=pltpu.VMEM)
    return pl.pallas_call(
        kernel,
        out_shape=jax.ShapeDtypeStruct((rows, 128), f32),
        in_specs=specs or [vmem] * len(args),
        out_specs=vmem,
        scratch_shapes=list(scratch),
        compiler_params=pltpu.CompilerParams(vmem_limit_bytes=24 * 1024 * 1024),
    )(*args)


def phase_tables(mode_beta, segment_kind):
    table = lax.dynamic_slice_in_dim(mode_beta, segment_kind[0], 1, 0)[0]
    low = lax.broadcasted_iota(jnp.int32, (SIDE, SIDE), 0)
    high = lax.broadcasted_iota(jnp.int32, (SIDE, SIDE), 1)
    index = low + SIDE * high
    signed = jnp.where(index < TOTAL // 2, index, index - TOTAL).astype(f32)
    omega = signed * (8.0 / TOTAL)
    phase = (
        table[:, 0, None, None] * omega
        + table[:, 1, None, None] * omega**2 / 2.0
        + table[:, 2, None, None] * omega**3 / 6.0
    )
    return jnp.stack([jnp.cos(phase), jnp.sin(phase)]) * (1.0 / TOTAL)


def by_pulse(field):
    return field.reshape(2, 8, 2, 16, 128).transpose(1, 0, 3, 2, 4).reshape(8, 64, 128)


def on_device(input_field, target_field, margin, pair_index, mode_beta, segment_kind):
    dft, twist = jnp.asarray(dft_parts()), jnp.asarray(twist_parts())
    phase = phase_tables(mode_beta, segment_kind)
    coupling = margin.reshape(2, 16, 2, 16).transpose(0, 3, 2, 1).reshape(8, 128)
    both = jnp.concatenate([by_pulse(input_field), by_pulse(target_field)], 1)
    both = lax.all_to_all(both, "tm", 0, 0, tiled=True).reshape(1024, 128)
    packed = call(forward_kernel, OWNERS * BLOCK, both, coupling, dft, twist, phase)
    packed = lax.all_to_all(packed.reshape(OWNERS, BLOCK, 128), "mode", 0, 0, tiled=True)
    vmem = pl.BlockSpec(memory_space=pltpu.VMEM)
    cotangent = call(
        kerr_kernel,
        512,
        pair_index,
        packed.reshape(OWNERS * BLOCK, 128),
        scratch=[pltpu.VMEM((256, 128), f32)] * 2,
        specs=[pl.BlockSpec(memory_space=pltpu.SMEM), vmem],
    )
    cotangent = lax.all_to_all(cotangent.reshape(OWNERS, 32, 128), "mode", 0, 0, tiled=True)
    gradient = call(backward_kernel, 512, cotangent.reshape(512, 128), dft, twist, phase)
    gradient = lax.all_to_all(gradient.reshape(8, 64, 128), "tm", 0, 0, tiled=True)
    gradient = gradient.reshape(8, 2, 16, 2, 128).transpose(1, 0, 3, 2, 4)
    return gradient.reshape(2, 8, 2, 2048)


def solution(mesh):
    field = P(None, "dp", "mode", "tm")
    return jax.shard_map(
        on_device,
        mesh=mesh,
        in_specs=(field, field, P("mode", None, None), P(), P(None, "mode", None), P()),
        out_specs=field,
        check_vma=False,
    )
```

profile of v0, /device:TPU:1, one launch (start us, length us, event | category | flops | bytes accessed | tf_op | source)
XLA Modules:
  0.0 76.9 jit_solution(17820319338496985985)
XLA Ops:
  0.0 0.0 copy-start
  0.0 1.2 %reshape.126 = f32[2,8,2,16,128]{4,3,2,1,0:T(8,128)S(1)} reshape(f32[2,8,2,2048]{3,2,1,0:T(2,128)} %param.8) | data formatting | bytes 524288 | tf_op jit(solution)/shard_map/reshape | solution.py:253
  1.2 0.0 copy-start.3
  1.2 0.1 copy.15
  1.3 0.8 %copy-done.3 = f32[2,8,2,2048]{3,2,1,0:T(2,128)S(1)} copy-done((f32[2,8,2,2048]{3,2,1,0:T(2,128)S(1)}, f32[2,8,2,2048]{3,2,1,0:T(2,128)}, u32[]{:S(2)}) %copy-start.3) | copy-done | bytes 262168
  2.1 0.2 reshape.128
  2.3 0.1 copy.16
  2.5 0.8 %pad_maximum_fusion = f32[8,128,128]{2,1,0:T(8,128)} fusion(f32[8,64,128]{2,1,0:T(8,128)S(1)} %bitcast.34, f32[8,64,128]{2,1,0:T(8,128)S(1)} %bitcast.33), kind=kLoop, calls=%fused_computation | loop fusion | flops 131072 | bytes 1048576 | tf_op jit(solution)/shard_map/concatenate | solution.py:260
  3.3 6.6 %all-to-all-start = ((f32[8,128,128]{2,1,0:T(8,128)}), f32[8,128,128]{2,1,0:T(8,128)S(1)}, u32[]{:S(2)}, u32[]{:S(2)}) async-start(f32[8,128,128]{2,1,0:T(8,128)} %pad_maximum_fusion), calls=%async_computation | async-start | bytes 1048576 | tf_op jit(solution)/shard_map/all_to_all | solution.py:261
  10.6 0.0 copy-done
  10.6 0.1 constant_dynamic-slice_fusion
  10.7 0.1 copy.19
  10.8 0.7 copy-done.4
  11.5 0.1 copy.17
  11.6 0.1 copy.18
  11.7 0.1 reshape.132.margin_ref
  11.8 0.2 slice_reduce_fusion.2
  12.0 0.6 fusion.1
  12.5 0.0 copy-start.1
  12.6 0.0 copy-start.2
  12.6 6.8 %all-to-all-done = f32[8,128,128]{2,1,0:T(8,128)S(1)} async-done(((f32[8,128,128]{2,1,0:T(8,128)}), f32[8,128,128]{2,1,0:T(8,128)S(1)}, u32[]{:S(2)}, u32[]{:S(2)}) %all-to-all-start) | async-done | bytes 524320 | tf_op jit(solution)/shard_map/all_to_all | solution.py:261
  19.5 0.0 copy-done.1
  19.5 0.0 copy-done.2
  19.5 2.5 %shard_map.82 = f32[1152,128]{1,0:T(8,128)} custom-call(f32[1024,128]{1,0:T(8,128)S(1)} %bitcast.25, f32[8,128]{1,0:T(8,128)S(1)} %reshape.132.margin_ref, bf16[4,128,128]{2,1,0:T(8,128)(2,1)S(1)} %copy-done.1, f32[2,128,128]{2,1,0:T(8,128)S(1)} %copy-done.2, f32[2,2,128,128]{3,2,1,0:T(8,128)S(1)} %maximum_multiply_fusion.phase_ref), custom_call_target="tpu_custom_call" | custom-call | tf_op jit(solution)/shard_map/pallas_call | solution.py:227
  22.0 7.6 %all-to-all-start.1 = ((f32[16,72,128]{2,1,0:T(8,128)}), f32[16,72,128]{2,1,0:T(8,128)S(1)}, u32[]{:S(2)}, u32[]{:S(2)}) async-start(f32[16,72,128]{2,1,0:T(8,128)} %bitcast.9), calls=%async_computation.1 | async-start | bytes 1179648 | tf_op jit(solution)/shard_map/all_to_all | solution.py:263
  29.6 0.1 copy.20.pair_ref
  29.7 17.0 %all-to-all-done.1 = f32[16,72,128]{2,1,0:T(8,128)S(1)} async-done(((f32[16,72,128]{2,1,0:T(8,128)}), f32[16,72,128]{2,1,0:T(8,128)S(1)}, u32[]{:S(2)}, u32[]{:S(2)}) %all-to-all-start.1) | async-done | bytes 589856 | tf_op jit(solution)/shard_map/all_to_all | solution.py:263
  46.7 3.6 %shard_map.83 = f32[512,128]{1,0:T(8,128)S(1)} custom-call(s32[16,2]{1,0:T(8,128)S(1)} %copy.20.pair_ref, f32[1152,128]{1,0:T(8,128)S(1)} %bitcast.24), custom_call_target="tpu_custom_call" | custom-call | tf_op jit(solution)/shard_map/pallas_call | solution.py:227
  50.3 12.8 %all_to_all.20 = f32[16,32,128]{2,1,0:T(8,128)S(1)} all-to-all(f32[16,32,128]{2,1,0:T(8,128)S(1)} %bitcast.26), channel_id=1, replica_groups=mesh['dp'=2,'mode'=16,'tm'=8] {'mode'}, dimensions={0} | all-to-all | bytes 524288 | tf_op jit(solution)/shard_map/all_to_all | solution.py:273
  63.2 1.7 %shard_map.84 = f32[512,128]{1,0:T(8,128)S(1)} custom-call(f32[512,128]{1,0:T(8,128)S(1)} %bitcast.27, bf16[4,128,128]{2,1,0:T(8,128)(2,1)S(1)} %copy-done.1, f32[2,128,128]{2,1,0:T(8,128)S(1)} %copy-done.2, f32[2,2,128,128]{3,2,1,0:T(8,128)S(1)} %maximum_multiply_fusion.phase_ref), custom_call_target="tpu_custom_call" | custom-call | tf_op jit(solution)/shard_map/pallas_call | solution.py:227
  64.9 11.2 %all_to_all.21 = f32[8,64,128]{2,1,0:T(8,128)S(1)} all-to-all(f32[8,64,128]{2,1,0:T(8,128)S(1)} %bitcast.28), channel_id=1, replica_groups=mesh['dp'=2,'mode'=16,'tm'=8] {'tm'}, dimensions={0} | all-to-all | bytes 524288 | tf_op jit(solution)/shard_map/all_to_all | solution.py:275
  76.0 0.8 %reshape.139 = f32[2,8,2,2048]{3,2,1,0:T(2,128)} reshape(f32[2,8,2,16,128]{4,3,2,1,0:T(8,128)S(1)} %bitcast.30) | data formatting | bytes 524288 | tf_op jit(solution)/shard_map/reshape | solution.py:277
  (7 shorter events, 0.1 us)
Async XLA Ops:
  0.0 10.6 %copy-start = (f32[1024,2,3]{0,1,2:T(2,128)S(1)}, f32[1024,2,3]{0,1,2:T(2,128)}, u32[]{:S(2)}) copy-start(f32[1024,2,3]{0,1,2:T(2,128)} %param.12) | copy-start | bytes 73732
  1.2 1.0 %copy-start.3 = (f32[2,8,2,2048]{3,2,1,0:T(2,128)S(1)}, f32[2,8,2,2048]{3,2,1,0:T(2,128)}, u32[]{:S(2)}) copy-start(f32[2,8,2,2048]{3,2,1,0:T(2,128)} %param.9) | copy-start | bytes 786436
  3.3 16.1 %all-to-all-start = ((f32[8,128,128]{2,1,0:T(8,128)}), f32[8,128,128]{2,1,0:T(8,128)S(1)}, u32[]{:S(2)}, u32[]{:S(2)}) async-start(f32[8,128,128]{2,1,0:T(8,128)} %pad_maximum_fusion), calls=%async_computation | async-start | bytes 1048576 | tf_op jit(solution)/shard_map/all_to_all | solution.py:261
  10.8 0.7 copy-start.4
  12.5 6.9 %copy-start.1 = (bf16[4,128,128]{2,1,0:T(8,128)(2,1)S(1)}, bf16[4,128,128]{2,1,0:T(8,128)(2,1)}, u32[]{:S(2)}) copy-start(bf16[4,128,128]{2,1,0:T(8,128)(2,1)} %constant.25.clone.dft_ref) | copy-start | bytes 393220
  12.6 6.9 %copy-start.2 = (f32[2,128,128]{2,1,0:T(8,128)S(1)}, f32[2,128,128]{2,1,0:T(8,128)}, u32[]{:S(2)}) copy-start(f32[2,128,128]{2,1,0:T(8,128)} %constant.26.clone.twist_ref) | copy-start | bytes 393220
  22.0 7.6 %copy-start.5 = (s32[16,2]{0,1:T(2,128)S(1)}, s32[16,2]{0,1:T(2,128)}, u32[]{:S(2)}) copy-start(s32[16,2]{0,1:T(2,128)} %param.11) | copy-start | bytes 388
  22.0 24.7 %all-to-all-start.1 = ((f32[16,72,128]{2,1,0:T(8,128)}), f32[16,72,128]{2,1,0:T(8,128)S(1)}, u32[]{:S(2)}, u32[]{:S(2)}) async-start(f32[16,72,128]{2,1,0:T(8,128)} %bitcast.9), calls=%async_computation.1 | async-start | bytes 1179648 | tf_op jit(solution)/shard_map/all_to_all | solution.py:263
where the time goes:
time: 77.3 us; the launch traced here: 76.9 us
  blocking collectives  24 us (31%)
  waiting for transfers between devices  23.9 us (31%)
  starting transfers between devices  14.3 us (18%)
  Pallas kernels  7.79 us (10%)
  local copies, waits for them, and re-layouts  4.73 us (6%)
  other arithmetic  1.45 us (2%)
  between operations  0.78 us (1%)
    all_to_all x1, waiting for transfers between devices, on_device(): lax.all_to_all(packed.reshape(OWNERS, BLOCK, 128), 'mode', 0, 0, tiled=True)  17 us
    all_to_all x1, blocking collectives, on_device(): lax.all_to_all(cotangent.reshape(OWNERS, 32, 128), 'mode', 0, 0, tiled=True)  12.8 us
    all_to_all x1, blocking collectives, on_device(): lax.all_to_all(gradient.reshape(8, 64, 128), 'tm', 0, 0, tiled=True)  11.2 us
    pallas_call x3, Pallas kernels, call(): pl.pallas_call(kernel, out_shape=jax.ShapeDtypeStruct((rows, 128), f32),...  7.79 us
    all_to_all x1, starting transfers between devices, on_device(): lax.all_to_all(packed.reshape(OWNERS, BLOCK, 128), 'mode', 0, 0, tiled=True)  7.63 us
    all_to_all x1, waiting for transfers between devices, on_device(): both = lax.all_to_all(both, 'tm', 0, 0, tiled=True).reshape(1024, 128)  6.85 us
    all_to_all x1, starting transfers between devices, on_device(): both = lax.all_to_all(both, 'tm', 0, 0, tiled=True).reshape(1024, 128)  6.63 us
    unnamed x14, local copies, waits for them, and re-layouts  1.67 us
  transfers between devices with their start and end apart: 2, of which 2 were waited for; matrix products, arithmetic and copies ran while one was open for 2% of the time, Pallas kernels for 0%

commit v1 on v0

--- a/solution.py
+++ b/solution.py
@@ -84,22 +84,108 @@
     return result
 
 
+def gather_kernel(
+    kind_ref, beta_hbm, margin_hbm, field_ref, target_ref,
+    out_ref, phase_ref, coupling_ref,
+    beta_ref, margin_ref, held_ref, small_sems, sems,
+):
+    small = [
+        pltpu.make_async_copy(there, here, small_sems.at[q])
+        for q, (there, here) in enumerate(
+            ((beta_hbm, beta_ref), (margin_hbm, margin_ref))
+        )
+    ]
+    for copy in small:
+        copy.start()
+    order = [(b, what) for b in range(8) for what in range(2)]
+    copies = {}
+    for b, what in order:
+        copies[b, what] = pltpu.make_async_copy(
+            (field_ref, target_ref)[what].at[:, b], held_ref.at[what, b], sems.at[what, b]
+        )
+        copies[b, what].start()
+    for copy in small:
+        copy.wait()
+
+    lane = lax.broadcasted_iota(jnp.int32, (128, 128), 1)
+    source = lax.broadcasted_iota(jnp.int32, (128, 128), 0)
+    place = source // 32 * 32 + source % 2 * 16 + source % 32 // 2
+    wide = jnp.zeros((16, 96), f32)
+    flat = []
+    for p in range(2):
+        rows = jnp.concatenate([margin_ref[p], wide], 1)
+        flat.append(
+            sum(
+                pltpu.roll(
+                    jnp.concatenate([rows[4 * q + jr : 4 * q + jr + 1] for q in range(4)], 0),
+                    32 * jr,
+                    1,
+                )
+                if jr
+                else jnp.concatenate([rows[4 * q : 4 * q + 1] for q in range(4)], 0)
+                for jr in range(4)
+            )
+        )
+    coupling_ref[...] = jnp.dot(
+        jnp.concatenate(flat, 0),
+        (place == lane).astype(f32),
+        precision=lax.Precision.HIGHEST,
+        preferred_element_type=f32,
+    )
+
+    kinds = lax.broadcasted_iota(jnp.int32, beta_ref.shape, 2)
+    table = jnp.sum(jnp.where(kinds == kind_ref[0], beta_ref[...], 0.0), axis=2, keepdims=True)
+    index = source + SIDE * lane
+    signed = jnp.where(index < TOTAL // 2, index, index - TOTAL).astype(f32)
+    omega = signed * (8.0 / TOTAL)
+    for m in range(2):
+        first, second, third = (table[q, m : m + 1] for q in range(3))
+        phase = first * omega + second * omega**2 / 2.0 + third * omega**3 / 6.0
+        phase_ref[0, m] = jnp.cos(phase) * (1.0 / TOTAL)
+        phase_ref[1, m] = jnp.sin(phase) * (1.0 / TOTAL)
+
+    for b, what in order:
+        copies[b, what].wait()
+        for part in range(2):
+            spot = b * 128 + what * 64 + part * 32
+            for k in range(16):
+                out_ref[pl.ds(spot + k, 2, stride=16), :] = held_ref[
+                    what, b, part, :, k * 128 : k * 128 + 128
+                ]
+
+
+def scatter_kernel(rows_ref, out_ref, held_ref, sems):
+    copies = []
+    for b in range(8):
+        for part in range(2):
+            for k in range(16):
+                held_ref[b, part, :, k * 128 : k * 128 + 128] = rows_ref[
+                    pl.ds(b * 64 + part * 32 + k, 2, stride=16), :
+                ]
+        copies.append(pltpu.make_async_copy(held_ref.at[b], out_ref.at[:, b], sems.at[b]))
+        copies[-1].start()
+    for copy in copies:
+        copy.wait()
+
+
 def forward_kernel(rows_ref, margin_ref, dft_ref, twist_ref, phase_ref, out_ref):
-    def series(what, m, part):
-        return [
-            rows_ref[pl.ds(s * 128 + what * 64 + part * 32 + m, 16, stride=2), :]
-            for s in range(TIMES)
-        ]
+    def chunk(s, what, m, part):
+        spot = s * 128 + what * 64 + part * 32 + m * 16
+        return rows_ref[spot : spot + 16, :]
 
     fields = [
-        tuple(jnp.concatenate(series(0, m, part), 0) for part in range(2)) for m in range(2)
+        tuple(
+            jnp.concatenate([chunk(s, 0, m, part) for s in range(TIMES)], 0) for part in range(2)
+        )
+        for m in range(2)
     ]
     for m in range(2):
         for part in range(2):
-            for s, chunk in enumerate(series(1, m, part)):
+            for s in range(TIMES):
+                rows = chunk(s, 1, m, part)
                 for h in range(2):
                     spot = (2 * s + h) * BLOCK + 32 + m * 16 + part * 8
-                    out_ref[spot : spot + 8, :] = chunk[8 * h : 8 * h + 8]
+                    out_ref[spot : spot + 8, :] = rows[8 * h : 8 * h + 8]
     margin = margin_ref[...]
     for k in range(OWNERS):
         out_ref[k * BLOCK + 64 : k * BLOCK + 72, :] = margin
@@ -129,12 +215,14 @@
     for m in range(2):
         for part in range(2):
             for s in range(TIMES):
-                out_ref[pl.ds(s * 64 + part * 32 + m, 16, stride=2), :] = result[m][part][
-                    16 * s : 16 * s + 16
-                ]
-
-
-def kerr_kernel(pair_ref, rows_ref, out_ref, w_ref, gw_ref):
+                spot = s * 64 + part * 32 + m * 16
+                out_ref[spot : spot + 16, :] = result[m][part][16 * s : 16 * s + 16]
+
+
+def kerr_kernel(pair_hbm, rows_ref, out_ref, pair_ref, w_ref, gw_ref, sem):
+    pairs_in = pltpu.make_async_copy(pair_hbm, pair_ref, sem)
+    pairs_in.start()
+
     def by_owner(row):
         return rows_ref[pl.ds(row, OWNERS, stride=BLOCK), :]
 
@@ -168,9 +256,10 @@
         [stacked(jnp.concatenate([q] * 4, 0).T) for q in quarters], 0
     )
 
+    pairs_in.wait()
     for j in range(PAIRS):
-        left = rows_ref[own_mode(pair_ref[j, 0], BLOCK), :]
-        right = rows_ref[own_mode(pair_ref[j, 1], BLOCK), :]
+        left = rows_ref[own_mode(pair_ref[0, j], BLOCK), :]
+        right = rows_ref[own_mode(pair_ref[1, j], BLOCK), :]
         lr, li, rr, ri = left[:8], left[8:], right[:8], right[8:]
         w_ref[j * 16 : j * 16 + 8, :] = lr * rr - li * ri
         w_ref[j * 16 + 8 : j * 16 + 16, :] = lr * ri + li * rr
@@ -214,67 +303,86 @@
     for j in range(PAIRS):
         gwr, gwi = gw_ref[j * 16 : j * 16 + 8, :], gw_ref[j * 16 + 8 : j * 16 + 16, :]
         for here, other in ((0, 1), (1, 0)):
-            factor = rows_ref[own_mode(pair_ref[j, other], BLOCK), :]
+            factor = rows_ref[own_mode(pair_ref[other, j], BLOCK), :]
             fr, fi = factor[:8], factor[8:]
-            spot = own_mode(pair_ref[j, here], 32)
+            spot = own_mode(pair_ref[here, j], 32)
             out_ref[spot, :] = out_ref[spot, :] + jnp.concatenate(
                 [gwr * fr + gwi * fi, gwi * fr - gwr * fi], 0
             )
 
 
-def call(kernel, rows, *args, scratch=(), specs=None):
-    vmem = pl.BlockSpec(memory_space=pltpu.VMEM)
-    return pl.pallas_call(
+VMEM, HBM = (pl.BlockSpec(memory_space=space) for space in (pltpu.VMEM, pltpu.HBM))
+
+
+def in_hbm(x):
+    return pltpu.with_memory_space_constraint(x, pltpu.HBM)
+
+
+def call(kernel, shapes, *args, scratch=(), specs=None, out=pltpu.VMEM):
+    shapes = [out(shape, f32) for shape in shapes]
+    results = pl.pallas_call(
         kernel,
-        out_shape=jax.ShapeDtypeStruct((rows, 128), f32),
-        in_specs=specs or [vmem] * len(args),
-        out_specs=vmem,
+        out_shape=shapes,
+        in_specs=specs or [VMEM] * len(args),
+        out_specs=[pl.BlockSpec(memory_space=out)] * len(shapes),
         scratch_shapes=list(scratch),
         compiler_params=pltpu.CompilerParams(vmem_limit_bytes=24 * 1024 * 1024),
     )(*args)
-
-
-def phase_tables(mode_beta, segment_kind):
-    table = lax.dynamic_slice_in_dim(mode_beta, segment_kind[0], 1, 0)[0]
-    low = lax.broadcasted_iota(jnp.int32, (SIDE, SIDE), 0)
-    high = lax.broadcasted_iota(jnp.int32, (SIDE, SIDE), 1)
-    index = low + SIDE * high
-    signed = jnp.where(index < TOTAL // 2, index, index - TOTAL).astype(f32)
-    omega = signed * (8.0 / TOTAL)
-    phase = (
-        table[:, 0, None, None] * omega
-        + table[:, 1, None, None] * omega**2 / 2.0
-        + table[:, 2, None, None] * omega**3 / 6.0
-    )
-    return jnp.stack([jnp.cos(phase), jnp.sin(phase)]) * (1.0 / TOTAL)
-
-
-def by_pulse(field):
-    return field.reshape(2, 8, 2, 16, 128).transpose(1, 0, 3, 2, 4).reshape(8, 64, 128)
+    return results if len(shapes) > 1 else results[0]
 
 
 def on_device(input_field, target_field, margin, pair_index, mode_beta, segment_kind):
     dft, twist = jnp.asarray(dft_parts()), jnp.asarray(twist_parts())
-    phase = phase_tables(mode_beta, segment_kind)
-    coupling = margin.reshape(2, 16, 2, 16).transpose(0, 3, 2, 1).reshape(8, 128)
-    both = jnp.concatenate([by_pulse(input_field), by_pulse(target_field)], 1)
-    both = lax.all_to_all(both, "tm", 0, 0, tiled=True).reshape(1024, 128)
-    packed = call(forward_kernel, OWNERS * BLOCK, both, coupling, dft, twist, phase)
+    both, phase, coupling = call(
+        gather_kernel,
+        [(1024, 128), (2, 2, SIDE, SIDE), (8, 128)],
+        segment_kind,
+        *map(
+            in_hbm,
+            (
+                mode_beta.transpose(2, 1, 0),
+                margin.transpose(0, 2, 1),
+                input_field,
+                target_field,
+            ),
+        ),
+        scratch=[
+            pltpu.VMEM((3, 2, mode_beta.shape[0]), f32),
+            pltpu.VMEM((2, PAIRS, MODES), f32),
+            pltpu.VMEM((2, 8, 2, 2, 2048), f32),
+            pltpu.SemaphoreType.DMA((2,)),
+            pltpu.SemaphoreType.DMA((2, 8)),
+        ],
+        specs=[pl.BlockSpec(memory_space=pltpu.SMEM)] + [HBM] * 4,
+    )
+    both = lax.all_to_all(both.reshape(8, 128, 128), "tm", 0, 0, tiled=True).reshape(1024, 128)
+    packed = call(forward_kernel, [(OWNERS * BLOCK, 128)], both, coupling, dft, twist, phase)
     packed = lax.all_to_all(packed.reshape(OWNERS, BLOCK, 128), "mode", 0, 0, tiled=True)
-    vmem = pl.BlockSpec(memory_space=pltpu.VMEM)
     cotangent = call(
         kerr_kernel,
-        512,
-        pair_index,
+        [(512, 128)],
+        in_hbm(pair_index.T),
         packed.reshape(OWNERS * BLOCK, 128),
-        scratch=[pltpu.VMEM((256, 128), f32)] * 2,
-        specs=[pl.BlockSpec(memory_space=pltpu.SMEM), vmem],
+        scratch=[
+            pltpu.SMEM((2, PAIRS), jnp.int32),
+            pltpu.VMEM((256, 128), f32),
+            pltpu.VMEM((256, 128), f32),
+            pltpu.SemaphoreType.DMA,
+        ],
+        specs=[HBM, VMEM],
     )
     cotangent = lax.all_to_all(cotangent.reshape(OWNERS, 32, 128), "mode", 0, 0, tiled=True)
-    gradient = call(backward_kernel, 512, cotangent.reshape(512, 128), dft, twist, phase)
+    gradient = call(
+        backward_kernel, [(512, 128)], cotangent.reshape(512, 128), dft, twist, phase
+    )
     gradient = lax.all_to_all(gradient.reshape(8, 64, 128), "tm", 0, 0, tiled=True)
-    gradient = gradient.reshape(8, 2, 16, 2, 128).transpose(1, 0, 3, 2, 4)
-    return gradient.reshape(2, 8, 2, 2048)
+    return call(
+        scatter_kernel,
+        [(2, 8, 2, 2048)],
+        gradient.reshape(512, 128),
+        scratch=[pltpu.VMEM((8, 2, 2, 2048), f32), pltpu.SemaphoreType.DMA((8,))],
+        out=pltpu.HBM,
+    )
 
 
 def solution(mesh):

time: 77.3 us -> 75.6 us (0.978)
  blocking collectives: 24 us -> 64.8 us
  waiting for transfers between devices: 23.9 us -> 0 us
  starting transfers between devices: 14.3 us -> 0 us
  local copies, waits for them, and re-layouts: 4.73 us -> 0.01 us
  Pallas kernels: 7.79 us -> 9.78 us
  other arithmetic: 1.45 us -> 0 us
    all_to_all x0 -> x2, blocking collectives: none -> 40.4 us  [the longest x1 25.1 us: on_device(): lax.all_to_all(packed.reshape(OWNERS, BLOCK, 128), 'mode', 0, 0, tiled=True)]
    all_to_all x2 -> x0, waiting for transfers between devices: 23.9 us -> none  [the longest x1 17 us: on_device(): lax.all_to_all(packed.reshape(OWNERS, BLOCK, 128), 'mode', 0, 0, tiled=True)]
    all_to_all x2 -> x0, starting transfers between devices: 14.3 us -> none  [the longest x1 7.63 us: on_device(): lax.all_to_all(packed.reshape(OWNERS, BLOCK, 128), 'mode', 0, 0, tiled=True)]
    reshape x5 -> x0, local copies, waits for them, and re-layouts: 2.34 us -> none  [the longest x2 1.38 us: by_pulse(): field.reshape(2, 8, 2, 16, 128).transpose(1, 0, 3, 2, 4).reshape(8, 64, 128)]
    pallas_call x3 -> x5, Pallas kernels: 7.79 us -> 9.78 us  [call(): pl.pallas_call(kernel, out_shape=shapes, in_specs=specs or [VMEM] * len(a...]
    unnamed x14 -> x4, local copies, waits for them, and re-layouts: 1.67 us -> 0.01 us
    concatenate x1 -> x0, other arithmetic: 0.83 us -> none  [on_device(): both = jnp.concatenate([by_pulse(input_field), by_pulse(target_field)], 1)]
  transfers between devices with their start and end apart: 2 -> 0, of which waited for: 2 -> 0; matrix products, arithmetic and copies ran while one was open for 2% -> 0% of each run, Pallas kernels for 0% -> 0%
where the time goes in v1:
time: 75.6 us; the launch traced here: 75.3 us
  blocking collectives  64.8 us (86%)
  Pallas kernels  9.78 us (13%)
    all_to_all x1, blocking collectives, on_device(): lax.all_to_all(packed.reshape(OWNERS, BLOCK, 128), 'mode', 0, 0, tiled=True)  25.1 us
    all_to_all x1, blocking collectives, on_device(): lax.all_to_all(both.reshape(8, 128, 128), 'tm', 0, 0, tiled=True)  15.3 us
    all_to_all x1, blocking collectives, on_device(): lax.all_to_all(cotangent.reshape(OWNERS, 32, 128), 'mode', 0, 0, tiled=True)  13.3 us
    all_to_all x1, blocking collectives, on_device(): lax.all_to_all(gradient.reshape(8, 64, 128), 'tm', 0, 0, tiled=True)  11.1 us
    pallas_call x5, Pallas kernels, call(): pl.pallas_call(kernel, out_shape=shapes, in_specs=specs or [VMEM] * len(a...  9.78 us

profile of v1, /device:TPU:1, one launch (start us, length us, event | category | flops | bytes accessed | tf_op | source)
XLA Modules:
  0.0 75.3 jit_solution(14660481940995239512)
XLA Ops:
  0.7 2.0 %shard_map.82 = (f32[1024,128]{1,0:T(8,128)S(1)}, f32[2,2,128,128]{3,2,1,0:T(8,128)S(1)}, f32[8,128]{1,0:T(8,128)S(1)}) custom-call(s32[1]{0:T(128)S(6)} %copy.9.kind_ref, f32[3,2,1024]{2,1,0:T(2,128)} %bitcast.19, f32[2,16,32]{2,1,0:T(8,128)} %bitcast.20, f32[2,8,2,2048]{3,2,1,0:T(2,128)} %field_ref.1, f32[2,8,2,2048]{3,2,1,0:T(2,128)} %target_ref.1), custom_call_target="tpu_custom_call" | custom-call | tf_op jit(solution)/shard_map/pallas_call | solution.py:323
  2.7 0.0 copy-start
  2.7 0.0 copy-start.1
  2.7 15.3 %all_to_all.20 = f32[8,128,128]{2,1,0:T(8,128)S(1)} all-to-all(f32[8,128,128]{2,1,0:T(8,128)S(1)} %bitcast.18), channel_id=1, replica_groups=mesh['dp'=2,'mode'=16,'tm'=8] {'tm'}, dimensions={0} | all-to-all | bytes 1048576 | tf_op jit(solution)/shard_map/all_to_all | solution.py:358
  17.9 0.0 copy-done
  18.0 0.0 copy-done.1
  18.0 1.7 %shard_map.83 = f32[1152,128]{1,0:T(8,128)S(1)} custom-call(f32[1024,128]{1,0:T(8,128)S(1)} %bitcast.13, f32[8,128]{1,0:T(8,128)S(1)} %get-tuple-element.9.margin_ref, bf16[4,128,128]{2,1,0:T(8,128)(2,1)S(1)} %copy-done.1, f32[2,128,128]{2,1,0:T(8,128)S(1)} %copy-done, f32[2,2,128,128]{3,2,1,0:T(8,128)S(1)} %get-tuple-element.10.phase_ref), custom_call_target="tpu_custom_call" | custom-call | tf_op jit(solution)/shard_map/pallas_call | solution.py:323
  19.6 25.1 %all_to_all.21 = f32[16,72,128]{2,1,0:T(8,128)S(1)} all-to-all(f32[16,72,128]{2,1,0:T(8,128)S(1)} %bitcast.11), channel_id=1, replica_groups=mesh['dp'=2,'mode'=16,'tm'=8] {'mode'}, dimensions={0} | all-to-all | bytes 1179648 | tf_op jit(solution)/shard_map/all_to_all | solution.py:360
  44.7 3.6 %shard_map.84 = f32[512,128]{1,0:T(8,128)S(1)} custom-call(s32[2,16]{1,0:T(2,128)} %bitcast.21, f32[1152,128]{1,0:T(8,128)S(1)} %bitcast.12), custom_call_target="tpu_custom_call" | custom-call | tf_op jit(solution)/shard_map/pallas_call | solution.py:323
  48.3 13.3 %all_to_all.22 = f32[16,32,128]{2,1,0:T(8,128)S(1)} all-to-all(f32[16,32,128]{2,1,0:T(8,128)S(1)} %bitcast.17), channel_id=1, replica_groups=mesh['dp'=2,'mode'=16,'tm'=8] {'mode'}, dimensions={0} | all-to-all | bytes 524288 | tf_op jit(solution)/shard_map/all_to_all | solution.py:374
  61.6 1.7 %shard_map.85 = f32[512,128]{1,0:T(8,128)S(1)} custom-call(f32[512,128]{1,0:T(8,128)S(1)} %bitcast.15, bf16[4,128,128]{2,1,0:T(8,128)(2,1)S(1)} %copy-done.1, f32[2,128,128]{2,1,0:T(8,128)S(1)} %copy-done, f32[2,2,128,128]{3,2,1,0:T(8,128)S(1)} %get-tuple-element.10.phase_ref), custom_call_target="tpu_custom_call" | custom-call | tf_op jit(solution)/shard_map/pallas_call | solution.py:323
  63.3 11.1 %all_to_all.23 = f32[8,64,128]{2,1,0:T(8,128)S(1)} all-to-all(f32[8,64,128]{2,1,0:T(8,128)S(1)} %bitcast.16), channel_id=1, replica_groups=mesh['dp'=2,'mode'=16,'tm'=8] {'tm'}, dimensions={0} | all-to-all | bytes 524288 | tf_op jit(solution)/shard_map/all_to_all | solution.py:378
  74.5 0.8 %shard_map.86 = f32[2,8,2,2048]{3,2,1,0:T(2,128)} custom-call(f32[512,128]{1,0:T(8,128)S(1)} %bitcast.14), custom_call_target="tpu_custom_call" | custom-call | tf_op jit(solution)/shard_map/pallas_call | solution.py:323
Async XLA Ops:
  2.7 15.3 %copy-start = (f32[2,128,128]{2,1,0:T(8,128)S(1)}, f32[2,128,128]{2,1,0:T(8,128)}, u32[]{:S(2)}) copy-start(f32[2,128,128]{2,1,0:T(8,128)} %constant.5.clone.twist_ref) | copy-start | bytes 393220
  2.7 15.3 %copy-start.1 = (bf16[4,128,128]{2,1,0:T(8,128)(2,1)S(1)}, bf16[4,128,128]{2,1,0:T(8,128)(2,1)}, u32[]{:S(2)}) copy-start(bf16[4,128,128]{2,1,0:T(8,128)(2,1)} %constant.4.clone.dft_ref) | copy-start | bytes 393220

commit v2 on v1

--- a/solution.py
+++ b/solution.py
@@ -66,33 +66,60 @@
             jnp.concatenate([form[0], form[0], form[1]], 0),
         )
 
+    def beside(parts):
+        return jnp.concatenate(parts, 1)
+
+    def below(parts):
+        return jnp.concatenate(parts, 0)
+
+    def quadrants(x):
+        return (x[:SIDE, :SIDE], x[SIDE:, :SIDE]), (x[:SIDE, SIDE:], x[SIDE:, SIDE:])
+
     tc, ts = twist[0], twist[1]
-    result = []
-    for m, (re, im) in enumerate(series):
+    y = quadrants(left(plus, beside([below(pair) for pair in series])))
+    y = below([beside([yr * tc + yi * ts, yi * tc - yr * ts]) for yr, yi in y])
+    z = right(minus, y)
+    turned = []
+    for m in range(2):
+        zr, zi = z[m * SIDE : (m + 1) * SIDE, :SIDE], z[m * SIDE : (m + 1) * SIDE, SIDE:]
         pc, ps = phase[0, m], sign * phase[1, m]
-        y = left(plus, jnp.concatenate([re, im], 0))
-        yr, yi = y[:SIDE], y[SIDE:]
-        y = jnp.concatenate([yr * tc + yi * ts, yi * tc - yr * ts], 1)
-        z = right(minus, y)
-        zr, zi = z[:, :SIDE], z[:, SIDE:]
-        z = jnp.concatenate([zr * pc - zi * ps, zr * ps + zi * pc], 1)
-        y = right(plus, z)
-        yr, yi = y[:, :SIDE], y[:, SIDE:]
-        y = jnp.concatenate([yr * tc - yi * ts, yr * ts + yi * tc], 0)
-        x = left(minus, y)
-        result.append((x[:SIDE], x[SIDE:]))
-    return result
+        turned.append(beside([zr * pc - zi * ps, zr * ps + zi * pc]))
+    y = right(plus, below(turned))
+    twisted = []
+    for m in range(2):
+        yr, yi = y[m * SIDE : (m + 1) * SIDE, :SIDE], y[m * SIDE : (m + 1) * SIDE, SIDE:]
+        twisted.append(below([yr * tc - yi * ts, yr * ts + yi * tc]))
+    return quadrants(left(minus, beside(twisted)))
+
+
+def cos_sin(angle):
+    turn = jnp.floor(angle * (2.0 / np.pi) + 0.5)
+    x = angle - turn * 1.5703125
+    x = x - turn * 4.837512969970703e-4
+    x = x - turn * 7.549789954891882e-8
+    z = x * x
+    sine = x + x * z * (-1.6666654611e-1 + z * (8.3321608736e-3 - z * 1.9515295891e-4))
+    cosine = 1.0 - 0.5 * z + z * z * (
+        4.166664568298827e-2 + z * (-1.388731625493765e-3 + z * 2.443315711809948e-5)
+    )
+    quarter = turn.astype(jnp.int32)
+    odd = quarter & 1 == 1
+    first, second = jnp.where(odd, sine, cosine), jnp.where(odd, cosine, sine)
+    return (
+        jnp.where((quarter + 1) & 2 == 2, -first, first),
+        jnp.where(quarter & 2 == 2, -second, second),
+    )
 
 
 def gather_kernel(
-    kind_ref, beta_hbm, margin_hbm, field_ref, target_ref,
-    out_ref, phase_ref, coupling_ref,
+    kind_ref, beta_hbm, margin_hbm, pair_hbm, field_ref, target_ref,
+    out_ref, phase_ref, coupling_ref, pair_ref,
     beta_ref, margin_ref, held_ref, small_sems, sems,
 ):
     small = [
         pltpu.make_async_copy(there, here, small_sems.at[q])
         for q, (there, here) in enumerate(
-            ((beta_hbm, beta_ref), (margin_hbm, margin_ref))
+            ((beta_hbm, beta_ref), (margin_hbm, margin_ref), (pair_hbm, pair_ref))
         )
     ]
     for copy in small:
@@ -104,8 +131,8 @@
             (field_ref, target_ref)[what].at[:, b], held_ref.at[what, b], sems.at[what, b]
         )
         copies[b, what].start()
-    for copy in small:
-        copy.wait()
+    small[0].wait()
+    small[1].wait()
 
     lane = lax.broadcasted_iota(jnp.int32, (128, 128), 1)
     source = lax.broadcasted_iota(jnp.int32, (128, 128), 0)
@@ -141,8 +168,9 @@
     for m in range(2):
         first, second, third = (table[q, m : m + 1] for q in range(3))
         phase = first * omega + second * omega**2 / 2.0 + third * omega**3 / 6.0
-        phase_ref[0, m] = jnp.cos(phase) * (1.0 / TOTAL)
-        phase_ref[1, m] = jnp.sin(phase) * (1.0 / TOTAL)
+        cosine, sine = cos_sin(phase)
+        phase_ref[0, m] = cosine * (1.0 / TOTAL)
+        phase_ref[1, m] = sine * (1.0 / TOTAL)
 
     for b, what in order:
         copies[b, what].wait()
@@ -152,6 +180,7 @@
                 out_ref[pl.ds(spot + k, 2, stride=16), :] = held_ref[
                     what, b, part, :, k * 128 : k * 128 + 128
                 ]
+    small[2].wait()
 
 
 def scatter_kernel(rows_ref, out_ref, held_ref, sems):
@@ -219,8 +248,8 @@
                 out_ref[spot : spot + 16, :] = result[m][part][16 * s : 16 * s + 16]
 
 
-def kerr_kernel(pair_hbm, rows_ref, out_ref, pair_ref, w_ref, gw_ref, sem):
-    pairs_in = pltpu.make_async_copy(pair_hbm, pair_ref, sem)
+def kerr_kernel(pair_vmem, rows_ref, out_ref, pair_ref, w_ref, gw_ref, other_ref, sem):
+    pairs_in = pltpu.make_async_copy(pair_vmem, pair_ref, sem)
     pairs_in.start()
 
     def by_owner(row):
@@ -235,6 +264,7 @@
         spot = (mode >> 1) * block + (mode & 1) * 16
         return pl.ds(pl.multiple_of(spot, 8), 16)
 
+    other_ref[...] = jnp.zeros_like(other_ref)
     lane = lax.broadcasted_iota(jnp.int32, (128, 128), 1)
 
     def stacked(x):
@@ -302,13 +332,14 @@
 
     for j in range(PAIRS):
         gwr, gwi = gw_ref[j * 16 : j * 16 + 8, :], gw_ref[j * 16 + 8 : j * 16 + 16, :]
-        for here, other in ((0, 1), (1, 0)):
+        for here, other, sum_ref in ((0, 1, out_ref), (1, 0, other_ref)):
             factor = rows_ref[own_mode(pair_ref[other, j], BLOCK), :]
             fr, fi = factor[:8], factor[8:]
             spot = own_mode(pair_ref[here, j], 32)
-            out_ref[spot, :] = out_ref[spot, :] + jnp.concatenate(
+            sum_ref[spot, :] = sum_ref[spot, :] + jnp.concatenate(
                 [gwr * fr + gwi * fi, gwi * fr - gwr * fi], 0
             )
+    out_ref[...] = out_ref[...] + other_ref[...]
 
 
 VMEM, HBM = (pl.BlockSpec(memory_space=space) for space in (pltpu.VMEM, pltpu.HBM))
@@ -319,7 +350,7 @@
 
 
 def call(kernel, shapes, *args, scratch=(), specs=None, out=pltpu.VMEM):
-    shapes = [out(shape, f32) for shape in shapes]
+    shapes = [out(shape, f32) if type(shape) is tuple else shape for shape in shapes]
     results = pl.pallas_call(
         kernel,
         out_shape=shapes,
@@ -333,15 +364,16 @@
 
 def on_device(input_field, target_field, margin, pair_index, mode_beta, segment_kind):
     dft, twist = jnp.asarray(dft_parts()), jnp.asarray(twist_parts())
-    both, phase, coupling = call(
+    both, phase, coupling, pairs = call(
         gather_kernel,
-        [(1024, 128), (2, 2, SIDE, SIDE), (8, 128)],
+        [(1024, 128), (2, 2, SIDE, SIDE), (8, 128), pltpu.VMEM((2, PAIRS), jnp.int32)],
         segment_kind,
         *map(
             in_hbm,
             (
                 mode_beta.transpose(2, 1, 0),
                 margin.transpose(0, 2, 1),
+                pair_index.T,
                 input_field,
                 target_field,
             ),
@@ -350,10 +382,10 @@
             pltpu.VMEM((3, 2, mode_beta.shape[0]), f32),
             pltpu.VMEM((2, PAIRS, MODES), f32),
             pltpu.VMEM((2, 8, 2, 2, 2048), f32),
-            pltpu.SemaphoreType.DMA((2,)),
+            pltpu.SemaphoreType.DMA((3,)),
             pltpu.SemaphoreType.DMA((2, 8)),
         ],
-        specs=[pl.BlockSpec(memory_space=pltpu.SMEM)] + [HBM] * 4,
+        specs=[pl.BlockSpec(memory_space=pltpu.SMEM)] + [HBM] * 5,
     )
     both = lax.all_to_all(both.reshape(8, 128, 128), "tm", 0, 0, tiled=True).reshape(1024, 128)
     packed = call(forward_kernel, [(OWNERS * BLOCK, 128)], both, coupling, dft, twist, phase)
@@ -361,15 +393,16 @@
     cotangent = call(
         kerr_kernel,
         [(512, 128)],
-        in_hbm(pair_index.T),
+        pairs,
         packed.reshape(OWNERS * BLOCK, 128),
         scratch=[
             pltpu.SMEM((2, PAIRS), jnp.int32),
             pltpu.VMEM((256, 128), f32),
             pltpu.VMEM((256, 128), f32),
+            pltpu.VMEM((512, 128), f32),
             pltpu.SemaphoreType.DMA,
         ],
-        specs=[HBM, VMEM],
+        specs=[VMEM, VMEM],
     )
     cotangent = lax.all_to_all(cotangent.reshape(OWNERS, 32, 128), "mode", 0, 0, tiled=True)
     gradient = call(

time: 75.6 us -> 74.2 us (0.981)
  Pallas kernels: 9.78 us -> 8.34 us
    pallas_call x5, Pallas kernels: 9.78 us -> 8.34 us  [call(): pl.pallas_call(kernel, out_shape=shapes, in_specs=specs or [VMEM] * len(a...]
where the time goes in v2:
time: 74.2 us; the launch traced here: 73.9 us
  blocking collectives  64.8 us (87%)
  Pallas kernels  8.34 us (11%)
    all_to_all x1, blocking collectives, on_device(): lax.all_to_all(packed.reshape(OWNERS, BLOCK, 128), 'mode', 0, 0, tiled=True)  25.1 us
    all_to_all x1, blocking collectives, on_device(): lax.all_to_all(both.reshape(8, 128, 128), 'tm', 0, 0, tiled=True)  15.3 us
    all_to_all x1, blocking collectives, on_device(): lax.all_to_all(cotangent.reshape(OWNERS, 32, 128), 'mode', 0, 0, tiled=True)  13.3 us
    all_to_all x1, blocking collectives, on_device(): lax.all_to_all(gradient.reshape(8, 64, 128), 'tm', 0, 0, tiled=True)  11.1 us
    pallas_call x5, Pallas kernels, call(): pl.pallas_call(kernel, out_shape=shapes, in_specs=specs or [VMEM] * len(a...  8.34 us

profile of v2, /device:TPU:1, one launch (start us, length us, event | category | flops | bytes accessed | tf_op | source)
XLA Modules:
  0.0 73.9 jit_solution(10049103950218574222)
XLA Ops:
  0.7 1.8 %shard_map.82 = (f32[1024,128]{1,0:T(8,128)S(1)}, f32[2,2,128,128]{3,2,1,0:T(8,128)S(1)}, f32[8,128]{1,0:T(8,128)S(1)}, s32[2,16]{1,0:T(2,128)S(1)}) custom-call(s32[1]{0:T(128)S(6)} %copy.9.kind_ref, f32[3,2,1024]{2,1,0:T(2,128)} %bitcast.19, f32[2,16,32]{2,1,0:T(8,128)} %bitcast.20, s32[2,16]{1,0:T(2,128)} %bitcast.21, f32[2,8,2,2048]{3,2,1,0:T(2,128)} %field_ref.1, ...), custom_call_target="tpu_custom_call" | custom-call | tf_op jit(solution)/shard_map/pallas_call | solution.py:354
  2.4 0.0 copy-start
  2.4 0.0 copy-start.1
  2.5 15.3 %all_to_all.20 = f32[8,128,128]{2,1,0:T(8,128)S(1)} all-to-all(f32[8,128,128]{2,1,0:T(8,128)S(1)} %bitcast.18), channel_id=1, replica_groups=mesh['dp'=2,'mode'=16,'tm'=8] {'tm'}, dimensions={0} | all-to-all | bytes 1048576 | tf_op jit(solution)/shard_map/all_to_all | solution.py:390
  17.7 0.0 copy-done
  17.7 0.0 copy-done.1
  17.7 1.2 %shard_map.83 = f32[1152,128]{1,0:T(8,128)S(1)} custom-call(f32[1024,128]{1,0:T(8,128)S(1)} %bitcast.13, f32[8,128]{1,0:T(8,128)S(1)} %get-tuple-element.11.margin_ref, bf16[4,128,128]{2,1,0:T(8,128)(2,1)S(1)} %copy-done.1, f32[2,128,128]{2,1,0:T(8,128)S(1)} %copy-done, f32[2,2,128,128]{3,2,1,0:T(8,128)S(1)} %get-tuple-element.12.phase_ref), custom_call_target="tpu_custom_call" | custom-call | tf_op jit(solution)/shard_map/pallas_call | solution.py:354
  19.0 25.1 %all_to_all.21 = f32[16,72,128]{2,1,0:T(8,128)S(1)} all-to-all(f32[16,72,128]{2,1,0:T(8,128)S(1)} %bitcast.11), channel_id=1, replica_groups=mesh['dp'=2,'mode'=16,'tm'=8] {'mode'}, dimensions={0} | all-to-all | bytes 1179648 | tf_op jit(solution)/shard_map/all_to_all | solution.py:392
  44.1 3.3 %shard_map.84 = f32[512,128]{1,0:T(8,128)S(1)} custom-call(s32[2,16]{1,0:T(2,128)S(1)} %get-tuple-element.9.pair_vmem, f32[1152,128]{1,0:T(8,128)S(1)} %bitcast.12), custom_call_target="tpu_custom_call" | custom-call | tf_op jit(solution)/shard_map/pallas_call | solution.py:354
  47.3 13.3 %all_to_all.22 = f32[16,32,128]{2,1,0:T(8,128)S(1)} all-to-all(f32[16,32,128]{2,1,0:T(8,128)S(1)} %bitcast.17), channel_id=1, replica_groups=mesh['dp'=2,'mode'=16,'tm'=8] {'mode'}, dimensions={0} | all-to-all | bytes 524288 | tf_op jit(solution)/shard_map/all_to_all | solution.py:407
  60.6 1.2 %shard_map.85 = f32[512,128]{1,0:T(8,128)S(1)} custom-call(f32[512,128]{1,0:T(8,128)S(1)} %bitcast.15, bf16[4,128,128]{2,1,0:T(8,128)(2,1)S(1)} %copy-done.1, f32[2,128,128]{2,1,0:T(8,128)S(1)} %copy-done, f32[2,2,128,128]{3,2,1,0:T(8,128)S(1)} %get-tuple-element.12.phase_ref), custom_call_target="tpu_custom_call" | custom-call | tf_op jit(solution)/shard_map/pallas_call | solution.py:354
  61.9 11.1 %all_to_all.23 = f32[8,64,128]{2,1,0:T(8,128)S(1)} all-to-all(f32[8,64,128]{2,1,0:T(8,128)S(1)} %bitcast.16), channel_id=1, replica_groups=mesh['dp'=2,'mode'=16,'tm'=8] {'tm'}, dimensions={0} | all-to-all | bytes 524288 | tf_op jit(solution)/shard_map/all_to_all | solution.py:411
  73.0 0.8 %shard_map.86 = f32[2,8,2,2048]{3,2,1,0:T(2,128)} custom-call(f32[512,128]{1,0:T(8,128)S(1)} %bitcast.14), custom_call_target="tpu_custom_call" | custom-call | tf_op jit(solution)/shard_map/pallas_call | solution.py:354
Async XLA Ops:
  2.4 15.3 %copy-start = (f32[2,128,128]{2,1,0:T(8,128)S(1)}, f32[2,128,128]{2,1,0:T(8,128)}, u32[]{:S(2)}) copy-start(f32[2,128,128]{2,1,0:T(8,128)} %constant.5.clone.twist_ref) | copy-start | bytes 393220
  2.4 15.3 %copy-start.1 = (bf16[4,128,128]{2,1,0:T(8,128)(2,1)S(1)}, bf16[4,128,128]{2,1,0:T(8,128)(2,1)}, u32[]{:S(2)}) copy-start(bf16[4,128,128]{2,1,0:T(8,128)(2,1)} %constant.4.clone.dft_ref) | copy-start | bytes 393220

commit v3 on v2

--- a/solution.py
+++ b/solution.py
@@ -113,8 +113,8 @@
 
 def gather_kernel(
     kind_ref, beta_hbm, margin_hbm, pair_hbm, field_ref, target_ref,
-    out_ref, phase_ref, coupling_ref, pair_ref,
-    beta_ref, margin_ref, held_ref, small_sems, sems,
+    out_ref, phase_ref, coupling_ref, spot_ref,
+    pair_ref, beta_ref, margin_ref, held_ref, small_sems, sems,
 ):
     small = [
         pltpu.make_async_copy(there, here, small_sems.at[q])
@@ -131,9 +131,20 @@
             (field_ref, target_ref)[what].at[:, b], held_ref.at[what, b], sems.at[what, b]
         )
         copies[b, what].start()
-    small[0].wait()
-    small[1].wait()
-
+
+    for b, what in order:
+        copies[b, what].wait()
+        for part in range(2):
+            spot = b * 128 + what * 64 + part * 32
+            for k in range(16):
+                out_ref[pl.ds(spot + k, 2, stride=16), :] = held_ref[
+                    what, b, part, :, k * 128 : k * 128 + 128
+                ]
+    for copy in small:
+        copy.wait()
+    pair = pair_ref[...]
+    for q, block in enumerate((BLOCK, 32)):
+        spot_ref[2 * q : 2 * q + 2, :] = (pair >> 1) * block + (pair & 1) * 16
     lane = lax.broadcasted_iota(jnp.int32, (128, 128), 1)
     source = lax.broadcasted_iota(jnp.int32, (128, 128), 0)
     place = source // 32 * 32 + source % 2 * 16 + source % 32 // 2
@@ -172,16 +183,6 @@
         phase_ref[0, m] = cosine * (1.0 / TOTAL)
         phase_ref[1, m] = sine * (1.0 / TOTAL)
 
-    for b, what in order:
-        copies[b, what].wait()
-        for part in range(2):
-            spot = b * 128 + what * 64 + part * 32
-            for k in range(16):
-                out_ref[pl.ds(spot + k, 2, stride=16), :] = held_ref[
-                    what, b, part, :, k * 128 : k * 128 + 128
-                ]
-    small[2].wait()
-
 
 def scatter_kernel(rows_ref, out_ref, held_ref, sems):
     copies = []
@@ -248,9 +249,9 @@
                 out_ref[spot : spot + 16, :] = result[m][part][16 * s : 16 * s + 16]
 
 
-def kerr_kernel(pair_vmem, rows_ref, out_ref, pair_ref, w_ref, gw_ref, other_ref, sem):
-    pairs_in = pltpu.make_async_copy(pair_vmem, pair_ref, sem)
-    pairs_in.start()
+def kerr_kernel(spot_vmem, rows_ref, out_ref, spot_ref, w_ref, gw_ref, other_ref, sem):
+    spots_in = pltpu.make_async_copy(spot_vmem, spot_ref, sem)
+    spots_in.start()
 
     def by_owner(row):
         return rows_ref[pl.ds(row, OWNERS, stride=BLOCK), :]
@@ -260,9 +261,8 @@
             [by_owner(first + m * 16 + part * 8 + s) for m in range(2)], 0
         )
 
-    def own_mode(mode, block):
-        spot = (mode >> 1) * block + (mode & 1) * 16
-        return pl.ds(pl.multiple_of(spot, 8), 16)
+    def mode_rows(kind, j):
+        return pl.ds(pl.multiple_of(spot_ref[kind, j], 8), 16)
 
     other_ref[...] = jnp.zeros_like(other_ref)
     lane = lax.broadcasted_iota(jnp.int32, (128, 128), 1)
@@ -286,10 +286,10 @@
         [stacked(jnp.concatenate([q] * 4, 0).T) for q in quarters], 0
     )
 
-    pairs_in.wait()
+    spots_in.wait()
     for j in range(PAIRS):
-        left = rows_ref[own_mode(pair_ref[0, j], BLOCK), :]
-        right = rows_ref[own_mode(pair_ref[1, j], BLOCK), :]
+        left = rows_ref[mode_rows(0, j), :]
+        right = rows_ref[mode_rows(1, j), :]
         lr, li, rr, ri = left[:8], left[8:], right[:8], right[8:]
         w_ref[j * 16 : j * 16 + 8, :] = lr * rr - li * ri
         w_ref[j * 16 + 8 : j * 16 + 16, :] = lr * ri + li * rr
@@ -333,9 +333,9 @@
     for j in range(PAIRS):
         gwr, gwi = gw_ref[j * 16 : j * 16 + 8, :], gw_ref[j * 16 + 8 : j * 16 + 16, :]
         for here, other, sum_ref in ((0, 1, out_ref), (1, 0, other_ref)):
-            factor = rows_ref[own_mode(pair_ref[other, j], BLOCK), :]
+            factor = rows_ref[mode_rows(other, j), :]
             fr, fi = factor[:8], factor[8:]
-            spot = own_mode(pair_ref[here, j], 32)
+            spot = mode_rows(2 + here, j)
             sum_ref[spot, :] = sum_ref[spot, :] + jnp.concatenate(
                 [gwr * fr + gwi * fi, gwi * fr - gwr * fi], 0
             )
@@ -364,9 +364,9 @@
 
 def on_device(input_field, target_field, margin, pair_index, mode_beta, segment_kind):
     dft, twist = jnp.asarray(dft_parts()), jnp.asarray(twist_parts())
-    both, phase, coupling, pairs = call(
+    both, phase, coupling, spots = call(
         gather_kernel,
-        [(1024, 128), (2, 2, SIDE, SIDE), (8, 128), pltpu.VMEM((2, PAIRS), jnp.int32)],
+        [(1024, 128), (2, 2, SIDE, SIDE), (8, 128), pltpu.VMEM((4, PAIRS), jnp.int32)],
         segment_kind,
         *map(
             in_hbm,
@@ -379,6 +379,7 @@
             ),
         ),
         scratch=[
+            pltpu.VMEM((2, PAIRS), jnp.int32),
             pltpu.VMEM((3, 2, mode_beta.shape[0]), f32),
             pltpu.VMEM((2, PAIRS, MODES), f32),
             pltpu.VMEM((2, 8, 2, 2, 2048), f32),
@@ -393,10 +394,10 @@
     cotangent = call(
         kerr_kernel,
         [(512, 128)],
-        pairs,
+        spots,
         packed.reshape(OWNERS * BLOCK, 128),
         scratch=[
-            pltpu.SMEM((2, PAIRS), jnp.int32),
+            pltpu.SMEM((4, PAIRS), jnp.int32),
             pltpu.VMEM((256, 128), f32),
             pltpu.VMEM((256, 128), f32),
             pltpu.VMEM((512, 128), f32),

time: 74.2 us -> 74 us (level)
  no operation moved by 1% of the time
where the time goes in v3:
time: 74 us; the launch traced here: 73.7 us
  blocking collectives  64.8 us (88%)
  Pallas kernels  8.18 us (11%)
    all_to_all x1, blocking collectives, on_device(): lax.all_to_all(packed.reshape(OWNERS, BLOCK, 128), 'mode', 0, 0, tiled=True)  25.1 us
    all_to_all x1, blocking collectives, on_device(): lax.all_to_all(both.reshape(8, 128, 128), 'tm', 0, 0, tiled=True)  15.3 us
    all_to_all x1, blocking collectives, on_device(): lax.all_to_all(cotangent.reshape(OWNERS, 32, 128), 'mode', 0, 0, tiled=True)  13.3 us
    all_to_all x1, blocking collectives, on_device(): lax.all_to_all(gradient.reshape(8, 64, 128), 'tm', 0, 0, tiled=True)  11.1 us
    pallas_call x5, Pallas kernels, call(): pl.pallas_call(kernel, out_shape=shapes, in_specs=specs or [VMEM] * len(a...  8.18 us

profile of v3, /device:TPU:1, one launch (start us, length us, event | category | flops | bytes accessed | tf_op | source)
XLA Modules:
  0.0 73.7 jit_solution(6697964301316206600)
XLA Ops:
  0.7 1.6 %shard_map.82 = (f32[1024,128]{1,0:T(8,128)S(1)}, f32[2,2,128,128]{3,2,1,0:T(8,128)S(1)}, f32[8,128]{1,0:T(8,128)S(1)}, s32[4,16]{1,0:T(4,128)S(1)}) custom-call(s32[1]{0:T(128)S(6)} %copy.9.kind_ref, f32[3,2,1024]{2,1,0:T(2,128)} %bitcast.19, f32[2,16,32]{2,1,0:T(8,128)} %bitcast.20, s32[2,16]{1,0:T(2,128)} %bitcast.21, f32[2,8,2,2048]{3,2,1,0:T(2,128)} %field_ref.1, ...), custom_call_target="tpu_custom_call" | custom-call | tf_op jit(solution)/shard_map/pallas_call | solution.py:354
  2.3 0.0 copy-start
  2.3 0.0 copy-start.1
  2.3 15.3 %all_to_all.20 = f32[8,128,128]{2,1,0:T(8,128)S(1)} all-to-all(f32[8,128,128]{2,1,0:T(8,128)S(1)} %bitcast.18), channel_id=1, replica_groups=mesh['dp'=2,'mode'=16,'tm'=8] {'tm'}, dimensions={0} | all-to-all | bytes 1048576 | tf_op jit(solution)/shard_map/all_to_all | solution.py:391
  17.5 0.0 copy-done
  17.5 0.0 copy-done.1
  17.5 1.2 %shard_map.83 = f32[1152,128]{1,0:T(8,128)S(1)} custom-call(f32[1024,128]{1,0:T(8,128)S(1)} %bitcast.13, f32[8,128]{1,0:T(8,128)S(1)} %get-tuple-element.11.margin_ref, bf16[4,128,128]{2,1,0:T(8,128)(2,1)S(1)} %copy-done.1, f32[2,128,128]{2,1,0:T(8,128)S(1)} %copy-done, f32[2,2,128,128]{3,2,1,0:T(8,128)S(1)} %get-tuple-element.12.phase_ref), custom_call_target="tpu_custom_call" | custom-call | tf_op jit(solution)/shard_map/pallas_call | solution.py:354
  18.8 25.1 %all_to_all.21 = f32[16,72,128]{2,1,0:T(8,128)S(1)} all-to-all(f32[16,72,128]{2,1,0:T(8,128)S(1)} %bitcast.11), channel_id=1, replica_groups=mesh['dp'=2,'mode'=16,'tm'=8] {'mode'}, dimensions={0} | all-to-all | bytes 1179648 | tf_op jit(solution)/shard_map/all_to_all | solution.py:393
  43.9 3.3 %shard_map.84 = f32[512,128]{1,0:T(8,128)S(1)} custom-call(s32[4,16]{1,0:T(4,128)S(1)} %get-tuple-element.9.spot_vmem, f32[1152,128]{1,0:T(8,128)S(1)} %bitcast.12), custom_call_target="tpu_custom_call" | custom-call | tf_op jit(solution)/shard_map/pallas_call | solution.py:354
  47.2 13.3 %all_to_all.22 = f32[16,32,128]{2,1,0:T(8,128)S(1)} all-to-all(f32[16,32,128]{2,1,0:T(8,128)S(1)} %bitcast.14), channel_id=1, replica_groups=mesh['dp'=2,'mode'=16,'tm'=8] {'mode'}, dimensions={0} | all-to-all | bytes 524288 | tf_op jit(solution)/shard_map/all_to_all | solution.py:408
  60.5 1.2 %shard_map.85 = f32[512,128]{1,0:T(8,128)S(1)} custom-call(f32[512,128]{1,0:T(8,128)S(1)} %bitcast.16, bf16[4,128,128]{2,1,0:T(8,128)(2,1)S(1)} %copy-done.1, f32[2,128,128]{2,1,0:T(8,128)S(1)} %copy-done, f32[2,2,128,128]{3,2,1,0:T(8,128)S(1)} %get-tuple-element.12.phase_ref), custom_call_target="tpu_custom_call" | custom-call | tf_op jit(solution)/shard_map/pallas_call | solution.py:354
  61.7 11.1 %all_to_all.23 = f32[8,64,128]{2,1,0:T(8,128)S(1)} all-to-all(f32[8,64,128]{2,1,0:T(8,128)S(1)} %bitcast.17), channel_id=1, replica_groups=mesh['dp'=2,'mode'=16,'tm'=8] {'tm'}, dimensions={0} | all-to-all | bytes 524288 | tf_op jit(solution)/shard_map/all_to_all | solution.py:412
  72.9 0.8 %shard_map.86 = f32[2,8,2,2048]{3,2,1,0:T(2,128)} custom-call(f32[512,128]{1,0:T(8,128)S(1)} %bitcast.15), custom_call_target="tpu_custom_call" | custom-call | tf_op jit(solution)/shard_map/pallas_call | solution.py:354
Async XLA Ops:
  2.3 15.3 %copy-start = (f32[2,128,128]{2,1,0:T(8,128)S(1)}, f32[2,128,128]{2,1,0:T(8,128)}, u32[]{:S(2)}) copy-start(f32[2,128,128]{2,1,0:T(8,128)} %constant.5.clone.twist_ref) | copy-start | bytes 393220
  2.3 15.3 %copy-start.1 = (bf16[4,128,128]{2,1,0:T(8,128)(2,1)S(1)}, bf16[4,128,128]{2,1,0:T(8,128)(2,1)}, u32[]{:S(2)}) copy-start(bf16[4,128,128]{2,1,0:T(8,128)(2,1)} %constant.4.clone.dft_ref) | copy-start | bytes 393220

commit v4 on v3

--- a/solution.py
+++ b/solution.py
@@ -76,18 +76,13 @@
         return (x[:SIDE, :SIDE], x[SIDE:, :SIDE]), (x[:SIDE, SIDE:], x[SIDE:, SIDE:])
 
     tc, ts = twist[0], twist[1]
-    y = quadrants(left(plus, beside([below(pair) for pair in series])))
-    y = below([beside([yr * tc + yi * ts, yi * tc - yr * ts]) for yr, yi in y])
-    z = right(minus, y)
-    turned = []
-    for m in range(2):
-        zr, zi = z[m * SIDE : (m + 1) * SIDE, :SIDE], z[m * SIDE : (m + 1) * SIDE, SIDE:]
+    twisted = []
+    for m, (yr, yi) in enumerate(quadrants(left(plus, beside([below(pair) for pair in series])))):
         pc, ps = phase[0, m], sign * phase[1, m]
-        turned.append(beside([zr * pc - zi * ps, zr * ps + zi * pc]))
-    y = right(plus, below(turned))
-    twisted = []
-    for m in range(2):
-        yr, yi = y[m * SIDE : (m + 1) * SIDE, :SIDE], y[m * SIDE : (m + 1) * SIDE, SIDE:]
+        z = right(minus, beside([yr * tc + yi * ts, yi * tc - yr * ts]))
+        zr, zi = z[:, :SIDE], z[:, SIDE:]
+        y = right(plus, beside([zr * pc - zi * ps, zr * ps + zi * pc]))
+        yr, yi = y[:, :SIDE], y[:, SIDE:]
         twisted.append(below([yr * tc - yi * ts, yr * ts + yi * tc]))
     return quadrants(left(minus, beside(twisted)))
 
@@ -294,6 +289,15 @@
         w_ref[j * 16 : j * 16 + 8, :] = lr * rr - li * ri
         w_ref[j * 16 + 8 : j * 16 + 16, :] = lr * ri + li * rr
 
+    eighth = lax.broadcasted_iota(jnp.int32, (8, 128), 0)
+
+    def over_vectors(x):
+        return x[:8] + x[8:16] + (x[16:24] + x[24:])
+
+    def merged(a, b, step):
+        mine = eighth & step == 0
+        return jnp.where(mine, a, b) + pltpu.roll(jnp.where(mine, b, a), step, 0)
+
     def operand(re, im):
         head, rest = heads(jnp.concatenate([re, im], 1))
         return jnp.concatenate([head, rest, head, rest], 0)
@@ -311,6 +315,7 @@
             total_im += cr * wi - ci * wr
         gr = 2.0 * (ur - kerr_scale * total_im - modes_at(32, 0, s))
         gi = 2.0 * (ui + kerr_scale * total_re - modes_at(32, 1, s))
+        sums = []
         spread = dot(second_form, operand(kerr_scale * gi, -kerr_scale * gr))
         for j in range(PAIRS):
             sr, si = spread[j * 32 : j * 32 + 32, :128], spread[j * 32 : j * 32 + 32, 128:]
@@ -318,12 +323,11 @@
             wi = w_ref[j * 16 + 8 + s : j * 16 + 9 + s, :]
             gr += sr * wr + si * wi
             gi += sr * wi - si * wr
-            gw_ref[j * 16 + s : j * 16 + s + 1, :] = jnp.sum(
-                sr * ur - si * ui, axis=0, keepdims=True
-            )
-            gw_ref[j * 16 + 8 + s : j * 16 + 9 + s, :] = jnp.sum(
-                sr * ui + si * ur, axis=0, keepdims=True
-            )
+            sums += [over_vectors(sr * ur - si * ui), over_vectors(sr * ui + si * ur)]
+            if len(sums) == 8:
+                for step in (1, 2, 4):
+                    sums = [merged(*two, step) for two in zip(sums[::2], sums[1::2])]
+                gw_ref[pl.ds((j - 3) * 16 + s, 8, stride=8), :] = sums.pop()
         for m in range(2):
             for part, g in enumerate((gr, gi)):
                 out_ref[pl.ds(m * 16 + part * 8 + s, OWNERS, stride=32), :] = g[

time: 74 us -> 73.7 us (level)
  no operation moved by 1% of the time
where the time goes in v4:
time: 73.7 us; the launch traced here: 73.4 us
  blocking collectives  64.8 us (88%)
  Pallas kernels  7.88 us (11%)
    all_to_all x1, blocking collectives, on_device(): lax.all_to_all(packed.reshape(OWNERS, BLOCK, 128), 'mode', 0, 0, tiled=True)  25.1 us
    all_to_all x1, blocking collectives, on_device(): lax.all_to_all(both.reshape(8, 128, 128), 'tm', 0, 0, tiled=True)  15.3 us
    all_to_all x1, blocking collectives, on_device(): lax.all_to_all(cotangent.reshape(OWNERS, 32, 128), 'mode', 0, 0, tiled=True)  13.3 us
    all_to_all x1, blocking collectives, on_device(): lax.all_to_all(gradient.reshape(8, 64, 128), 'tm', 0, 0, tiled=True)  11.1 us
    pallas_call x5, Pallas kernels, call(): pl.pallas_call(kernel, out_shape=shapes, in_specs=specs or [VMEM] * len(a...  7.88 us

profile of v4, /device:TPU:1, one launch (start us, length us, event | category | flops | bytes accessed | tf_op | source)
XLA Modules:
  0.0 73.4 jit_solution(6855657028149231476)
XLA Ops:
  0.7 1.6 %shard_map.82 = (f32[1024,128]{1,0:T(8,128)S(1)}, f32[2,2,128,128]{3,2,1,0:T(8,128)S(1)}, f32[8,128]{1,0:T(8,128)S(1)}, s32[4,16]{1,0:T(4,128)S(1)}) custom-call(s32[1]{0:T(128)S(6)} %copy.9.kind_ref, f32[3,2,1024]{2,1,0:T(2,128)} %bitcast.19, f32[2,16,32]{2,1,0:T(8,128)} %bitcast.20, s32[2,16]{1,0:T(2,128)} %bitcast.21, f32[2,8,2,2048]{3,2,1,0:T(2,128)} %field_ref.1, ...), custom_call_target="tpu_custom_call" | custom-call | tf_op jit(solution)/shard_map/pallas_call | solution.py:358
  2.3 0.0 copy-start
  2.3 0.0 copy-start.1
  2.3 15.3 %all_to_all.20 = f32[8,128,128]{2,1,0:T(8,128)S(1)} all-to-all(f32[8,128,128]{2,1,0:T(8,128)S(1)} %bitcast.18), channel_id=1, replica_groups=mesh['dp'=2,'mode'=16,'tm'=8] {'tm'}, dimensions={0} | all-to-all | bytes 1048576 | tf_op jit(solution)/shard_map/all_to_all | solution.py:395
  17.5 0.0 copy-done
  17.5 0.0 copy-done.1
  17.5 1.1 %shard_map.83 = f32[1152,128]{1,0:T(8,128)S(1)} custom-call(f32[1024,128]{1,0:T(8,128)S(1)} %bitcast.13, f32[8,128]{1,0:T(8,128)S(1)} %get-tuple-element.11.margin_ref, bf16[4,128,128]{2,1,0:T(8,128)(2,1)S(1)} %copy-done.1, f32[2,128,128]{2,1,0:T(8,128)S(1)} %copy-done, f32[2,2,128,128]{3,2,1,0:T(8,128)S(1)} %get-tuple-element.12.phase_ref), custom_call_target="tpu_custom_call" | custom-call | tf_op jit(solution)/shard_map/pallas_call | solution.py:358
  18.7 25.1 %all_to_all.21 = f32[16,72,128]{2,1,0:T(8,128)S(1)} all-to-all(f32[16,72,128]{2,1,0:T(8,128)S(1)} %bitcast.11), channel_id=1, replica_groups=mesh['dp'=2,'mode'=16,'tm'=8] {'mode'}, dimensions={0} | all-to-all | bytes 1179648 | tf_op jit(solution)/shard_map/all_to_all | solution.py:397
  43.8 3.2 %shard_map.84 = f32[512,128]{1,0:T(8,128)S(1)} custom-call(s32[4,16]{1,0:T(4,128)S(1)} %get-tuple-element.9.spot_vmem, f32[1152,128]{1,0:T(8,128)S(1)} %bitcast.12), custom_call_target="tpu_custom_call" | custom-call | tf_op jit(solution)/shard_map/pallas_call | solution.py:358
  47.0 13.3 %all_to_all.22 = f32[16,32,128]{2,1,0:T(8,128)S(1)} all-to-all(f32[16,32,128]{2,1,0:T(8,128)S(1)} %bitcast.14), channel_id=1, replica_groups=mesh['dp'=2,'mode'=16,'tm'=8] {'mode'}, dimensions={0} | all-to-all | bytes 524288 | tf_op jit(solution)/shard_map/all_to_all | solution.py:412
  60.3 1.1 %shard_map.85 = f32[512,128]{1,0:T(8,128)S(1)} custom-call(f32[512,128]{1,0:T(8,128)S(1)} %bitcast.16, bf16[4,128,128]{2,1,0:T(8,128)(2,1)S(1)} %copy-done.1, f32[2,128,128]{2,1,0:T(8,128)S(1)} %copy-done, f32[2,2,128,128]{3,2,1,0:T(8,128)S(1)} %get-tuple-element.12.phase_ref), custom_call_target="tpu_custom_call" | custom-call | tf_op jit(solution)/shard_map/pallas_call | solution.py:358
  61.4 11.1 %all_to_all.23 = f32[8,64,128]{2,1,0:T(8,128)S(1)} all-to-all(f32[8,64,128]{2,1,0:T(8,128)S(1)} %bitcast.17), channel_id=1, replica_groups=mesh['dp'=2,'mode'=16,'tm'=8] {'tm'}, dimensions={0} | all-to-all | bytes 524288 | tf_op jit(solution)/shard_map/all_to_all | solution.py:416
  72.6 0.8 %shard_map.86 = f32[2,8,2,2048]{3,2,1,0:T(2,128)} custom-call(f32[512,128]{1,0:T(8,128)S(1)} %bitcast.15), custom_call_target="tpu_custom_call" | custom-call | tf_op jit(solution)/shard_map/pallas_call | solution.py:358
Async XLA Ops:
  2.3 15.3 %copy-start = (f32[2,128,128]{2,1,0:T(8,128)S(1)}, f32[2,128,128]{2,1,0:T(8,128)}, u32[]{:S(2)}) copy-start(f32[2,128,128]{2,1,0:T(8,128)} %constant.5.clone.twist_ref) | copy-start | bytes 393220
  2.3 15.3 %copy-start.1 = (bf16[4,128,128]{2,1,0:T(8,128)(2,1)S(1)}, bf16[4,128,128]{2,1,0:T(8,128)(2,1)}, u32[]{:S(2)}) copy-start(bf16[4,128,128]{2,1,0:T(8,128)(2,1)} %constant.4.clone.dft_ref) | copy-start | bytes 393220

commit v5 on v4

--- a/solution.py
+++ b/solution.py
@@ -302,9 +302,13 @@
         head, rest = heads(jnp.concatenate([re, im], 1))
         return jnp.concatenate([head, rest, head, rest], 0)
 
+    def coupled_at(s):
+        ur, ui = modes_at(0, 0, s), modes_at(0, 1, s)
+        return ur, ui, dot(first_form, operand(ur, ui))
+
+    later = coupled_at(0)
     for s in range(8):
-        ur, ui = modes_at(0, 0, s), modes_at(0, 1, s)
-        coupled = dot(first_form, operand(ur, ui))
+        ur, ui, coupled = later
         total_re = total_im = 0.0
         for j in range(PAIRS):
             row = ((j % 4) * 4 + j // 4) * 32
@@ -317,6 +321,8 @@
         gi = 2.0 * (ui + kerr_scale * total_re - modes_at(32, 1, s))
         sums = []
         spread = dot(second_form, operand(kerr_scale * gi, -kerr_scale * gr))
+        if s < 7:
+            later = coupled_at(s + 1)
         for j in range(PAIRS):
             sr, si = spread[j * 32 : j * 32 + 32, :128], spread[j * 32 : j * 32 + 32, 128:]
             wr = w_ref[j * 16 + s : j * 16 + s + 1, :]

time: 73.7 us -> 73.7 us (level)
  no operation moved by 1% of the time
where the time goes in v5:
time: 73.7 us; the launch traced here: 73.4 us
  blocking collectives  64.8 us (88%)
  Pallas kernels  7.88 us (11%)
    all_to_all x1, blocking collectives, on_device(): lax.all_to_all(packed.reshape(OWNERS, BLOCK, 128), 'mode', 0, 0, tiled=True)  25.1 us
    all_to_all x1, blocking collectives, on_device(): lax.all_to_all(both.reshape(8, 128, 128), 'tm', 0, 0, tiled=True)  15.3 us
    all_to_all x1, blocking collectives, on_device(): lax.all_to_all(cotangent.reshape(OWNERS, 32, 128), 'mode', 0, 0, tiled=True)  13.3 us
    all_to_all x1, blocking collectives, on_device(): lax.all_to_all(gradient.reshape(8, 64, 128), 'tm', 0, 0, tiled=True)  11.2 us
    pallas_call x5, Pallas kernels, call(): pl.pallas_call(kernel, out_shape=shapes, in_specs=specs or [VMEM] * len(a...  7.88 us

profile of v5, /device:TPU:1, one launch (start us, length us, event | category | flops | bytes accessed | tf_op | source)
XLA Modules:
  0.0 73.4 jit_solution(6855657028149231476)
XLA Ops:
  0.7 1.6 %shard_map.82 = (f32[1024,128]{1,0:T(8,128)S(1)}, f32[2,2,128,128]{3,2,1,0:T(8,128)S(1)}, f32[8,128]{1,0:T(8,128)S(1)}, s32[4,16]{1,0:T(4,128)S(1)}) custom-call(s32[1]{0:T(128)S(6)} %copy.9.kind_ref, f32[3,2,1024]{2,1,0:T(2,128)} %bitcast.19, f32[2,16,32]{2,1,0:T(8,128)} %bitcast.20, s32[2,16]{1,0:T(2,128)} %bitcast.21, f32[2,8,2,2048]{3,2,1,0:T(2,128)} %field_ref.1, ...), custom_call_target="tpu_custom_call" | custom-call | tf_op jit(solution)/shard_map/pallas_call | solution.py:364
  2.3 0.0 copy-start
  2.3 0.0 copy-start.1
  2.3 15.3 %all_to_all.20 = f32[8,128,128]{2,1,0:T(8,128)S(1)} all-to-all(f32[8,128,128]{2,1,0:T(8,128)S(1)} %bitcast.18), channel_id=1, replica_groups=mesh['dp'=2,'mode'=16,'tm'=8] {'tm'}, dimensions={0} | all-to-all | bytes 1048576 | tf_op jit(solution)/shard_map/all_to_all | solution.py:401
  17.5 0.0 copy-done
  17.5 0.0 copy-done.1
  17.5 1.1 %shard_map.83 = f32[1152,128]{1,0:T(8,128)S(1)} custom-call(f32[1024,128]{1,0:T(8,128)S(1)} %bitcast.13, f32[8,128]{1,0:T(8,128)S(1)} %get-tuple-element.11.margin_ref, bf16[4,128,128]{2,1,0:T(8,128)(2,1)S(1)} %copy-done.1, f32[2,128,128]{2,1,0:T(8,128)S(1)} %copy-done, f32[2,2,128,128]{3,2,1,0:T(8,128)S(1)} %get-tuple-element.12.phase_ref), custom_call_target="tpu_custom_call" | custom-call | tf_op jit(solution)/shard_map/pallas_call | solution.py:364
  18.7 25.1 %all_to_all.21 = f32[16,72,128]{2,1,0:T(8,128)S(1)} all-to-all(f32[16,72,128]{2,1,0:T(8,128)S(1)} %bitcast.11), channel_id=1, replica_groups=mesh['dp'=2,'mode'=16,'tm'=8] {'mode'}, dimensions={0} | all-to-all | bytes 1179648 | tf_op jit(solution)/shard_map/all_to_all | solution.py:403
  43.8 3.2 %shard_map.84 = f32[512,128]{1,0:T(8,128)S(1)} custom-call(s32[4,16]{1,0:T(4,128)S(1)} %get-tuple-element.9.spot_vmem, f32[1152,128]{1,0:T(8,128)S(1)} %bitcast.12), custom_call_target="tpu_custom_call" | custom-call | tf_op jit(solution)/shard_map/pallas_call | solution.py:364
  47.0 13.3 %all_to_all.22 = f32[16,32,128]{2,1,0:T(8,128)S(1)} all-to-all(f32[16,32,128]{2,1,0:T(8,128)S(1)} %bitcast.14), channel_id=1, replica_groups=mesh['dp'=2,'mode'=16,'tm'=8] {'mode'}, dimensions={0} | all-to-all | bytes 524288 | tf_op jit(solution)/shard_map/all_to_all | solution.py:418
  60.3 1.1 %shard_map.85 = f32[512,128]{1,0:T(8,128)S(1)} custom-call(f32[512,128]{1,0:T(8,128)S(1)} %bitcast.16, bf16[4,128,128]{2,1,0:T(8,128)(2,1)S(1)} %copy-done.1, f32[2,128,128]{2,1,0:T(8,128)S(1)} %copy-done, f32[2,2,128,128]{3,2,1,0:T(8,128)S(1)} %get-tuple-element.12.phase_ref), custom_call_target="tpu_custom_call" | custom-call | tf_op jit(solution)/shard_map/pallas_call | solution.py:364
  61.4 11.2 %all_to_all.23 = f32[8,64,128]{2,1,0:T(8,128)S(1)} all-to-all(f32[8,64,128]{2,1,0:T(8,128)S(1)} %bitcast.17), channel_id=1, replica_groups=mesh['dp'=2,'mode'=16,'tm'=8] {'tm'}, dimensions={0} | all-to-all | bytes 524288 | tf_op jit(solution)/shard_map/all_to_all | solution.py:422
  72.6 0.8 %shard_map.86 = f32[2,8,2,2048]{3,2,1,0:T(2,128)} custom-call(f32[512,128]{1,0:T(8,128)S(1)} %bitcast.15), custom_call_target="tpu_custom_call" | custom-call | tf_op jit(solution)/shard_map/pallas_call | solution.py:364
Async XLA Ops:
  2.3 15.3 %copy-start = (f32[2,128,128]{2,1,0:T(8,128)S(1)}, f32[2,128,128]{2,1,0:T(8,128)}, u32[]{:S(2)}) copy-start(f32[2,128,128]{2,1,0:T(8,128)} %constant.5.clone.twist_ref) | copy-start | bytes 393220
  2.3 15.3 %copy-start.1 = (bf16[4,128,128]{2,1,0:T(8,128)(2,1)S(1)}, bf16[4,128,128]{2,1,0:T(8,128)(2,1)}, u32[]{:S(2)}) copy-start(bf16[4,128,128]{2,1,0:T(8,128)(2,1)} %constant.4.clone.dft_ref) | copy-start | bytes 393220
